TPU v7x, 32 devices: a whole 2x2x4 slice. The times are simulated.
32 devices in a mesh: rep: 2 (over y), frame: 16 (over z, x, core).
Axes of the slice: x: 2, y: 2, z: 4, core: 2. Of those that a mesh axis runs over, the one named last changes fastest.
Arguments:
- frames: bfloat16 [4096, 512], P(('rep', 'frame')), parts along dimension 0, may hold values from -6 to 6
- segment: int32 [4096], P(('rep', 'frame')), parts along dimension 0, may hold values from 0 to 8, as said below
- latents: bfloat16 [2048, 1024], P('frame'), may hold values from -1.5 to 1.5
- latent_queries: bfloat16 [2048, 1024], P('frame'), may hold values from -240 to 240
- w_kv: bfloat16 [512, 2048], replicated, may hold values from -0.25 to 0.25
- w_cross_out: bfloat16 [1024, 1024], replicated, may hold values from -0.1875 to 0.1875
- w_self_qkv: bfloat16 [1024, 3072], replicated
- w_self_out: bfloat16 [1024, 1024], replicated, may hold values from -0.1875 to 0.1875
Outputs:
- encoded: bfloat16 [4096, 1024], P(('rep', 'frame')), parts along dimension 0
There are 2 independent parts, one for each index of `rep`. A program takes and returns all parts, laid end to end along the dimension named above; an argument that names none is the same for every part. Nothing has to cross between parts.
Inputs may be any that keep to these rules, and one draw needn't show every extreme that they name: `segment`: ids are constant over aligned runs of 64 frames; 0 marks silence; every id from 1 to 8 labels some frame; the share of silent frames differs between regions of the recording.
All inputs are finite; a program needn't handle non-finite values.
Results may differ from a plain program's by a relative error of at most 0.014.
The roundings to bfloat16 on the way count: a program that leaves them out, or rounds other values in their place, can miss the bound.
Values may be sent and summed in bfloat16 or wider, within the bound.
A program may use at most 128 MiB of HBM per device.

v0:
```python
import math

import jax
import jax.numpy as jnp
from jax import lax
from jax.sharding import PartitionSpec as P

H = 16
HEAD_DIM = 64
L = 2048
NB = 8


NEG = -1e30


def layer_norm(inputs):
    centre = inputs - jnp.mean(inputs, axis=-1, keepdims=True)
    spread = jnp.mean(centre * centre, axis=-1, keepdims=True)
    return centre * lax.rsqrt(spread + 1e-05)


def shards(frames, segment, latents, latent_queries, w_kv, w_cross_out, w_self_qkv, w_self_out):
    feature_width = w_kv.shape[1] // 2
    owned_rows = latents.shape[0]
    frame_count = frames.shape[0]
    scale = 1.0 / math.sqrt(HEAD_DIM)
    block_rows = L // NB
    latent_full = latents.astype(jnp.float32)
    normed = layer_norm(frames.astype(jnp.float32)).astype(jnp.bfloat16)
    keyval = jnp.dot(normed, w_kv, preferred_element_type=jnp.float32).astype(jnp.bfloat16)
    key_heads = keyval[:, :feature_width].reshape(frame_count, H, HEAD_DIM).transpose(1, 0, 2)
    value_heads = keyval[:, feature_width:].reshape(frame_count, H, HEAD_DIM).transpose(1, 0, 2)
    total_rows = owned_rows * lax.axis_size("frame")
    piece = lax.all_gather(latent_queries, "frame", axis=0, tiled=True)
    piece_rows = piece.shape[0]
    block_ids = jnp.arange(piece_rows, dtype=jnp.int32) // block_rows + 1
    allowed = segment[None, :] == block_ids[:, None]
    query_heads = piece.reshape(piece_rows, H, HEAD_DIM).transpose(1, 0, 2)

    def one_head(item):
        query_head, key_head, value_head = item
        score = (
            jnp.einsum("re,fe->rf", query_head, key_head, preferred_element_type=jnp.float32)
            * scale
        )
        score = jnp.where(allowed, score, NEG)
        block_max = jnp.max(score, axis=1)
        weights = jnp.where(allowed, jnp.exp(score - block_max[:, None]), 0.0)
        block_total = jnp.sum(weights, axis=1)
        summed = jnp.dot(
            weights.astype(jnp.bfloat16), value_head, preferred_element_type=jnp.float32
        )
        return (block_max, block_total, summed)

    block_max, block_total, summed = lax.map(one_head, (query_heads, key_heads, value_heads))
    run_max = block_max.T
    run_total = block_total.T
    joined = summed.transpose(1, 0, 2).reshape(piece_rows, feature_width)
    run_acc = joined
    run_max, run_total, run_acc = (run_max, run_total, run_acc)
    sources = lax.axis_size("frame")
    got_acc, got_max, got_total = (
        lax.all_to_all(
            run_acc.reshape(sources, owned_rows, feature_width),
            "frame",
            split_axis=0,
            concat_axis=0,
            tiled=True,
        ),
        lax.all_to_all(
            run_max.reshape(sources, owned_rows, H),
            "frame",
            split_axis=0,
            concat_axis=0,
            tiled=True,
        ),
        lax.all_to_all(
            run_total.reshape(sources, owned_rows, H),
            "frame",
            split_axis=0,
            concat_axis=0,
            tiled=True,
        ),
    )
    global_max = jnp.max(got_max, axis=0)
    factor = jnp.exp(got_max - global_max[None])
    norms = jnp.sum(got_total * factor, axis=0)
    sums = jnp.sum(
        got_acc.reshape(sources, owned_rows, H, HEAD_DIM) * factor[:, :, :, None], axis=0
    )
    cross = (sums / norms[:, :, None]).reshape(owned_rows, feature_width)
    cross = cross.astype(jnp.bfloat16)
    mixed = latent_full + jnp.dot(cross, w_cross_out, preferred_element_type=jnp.float32)
    normed_latent = layer_norm(mixed).astype(jnp.bfloat16)
    triple = jnp.dot(normed_latent, w_self_qkv, preferred_element_type=jnp.float32).astype(
        jnp.bfloat16
    )
    self_query = triple[:, :feature_width].reshape(owned_rows, H, HEAD_DIM)
    self_key = triple[:, feature_width : 2 * feature_width]
    self_value = triple[:, 2 * feature_width :]
    every_key, every_value = (
        lax.all_gather(self_key, "frame", axis=0, tiled=True),
        lax.all_gather(self_value, "frame", axis=0, tiled=True),
    )
    every_key = every_key.reshape(total_rows, H, HEAD_DIM)
    every_value = every_value.reshape(total_rows, H, HEAD_DIM)
    score = (
        jnp.einsum("rhe,mhe->hrm", self_query, every_key, preferred_element_type=jnp.float32)
        * scale
    )
    peak = jnp.max(score, axis=2, keepdims=True)
    expo = jnp.exp(score - peak)
    probs = (expo / jnp.sum(expo, axis=2, keepdims=True)).astype(jnp.bfloat16)
    attended = jnp.einsum("hrm,mhe->rhe", probs, every_value, preferred_element_type=jnp.float32)
    attended = attended.reshape(owned_rows, feature_width).astype(jnp.bfloat16)
    return (mixed + jnp.dot(attended, w_self_out, preferred_element_type=jnp.float32)).astype(
        jnp.bfloat16
    )


def solution(mesh):
    placed = (
        P(("rep", "frame"), None),
        P(("rep", "frame")),
        P("frame", None),
        P("frame", None),
        P(),
        P(),
        P(),
        P(),
    )
    return jax.shard_map(
        shards, mesh=mesh, in_specs=placed, out_specs=P(("rep", "frame"), None), check_vma=False
    )
```

profile of v0, /device:TPU:0, one launch (start us, length us, event | category | flops | bytes accessed | tf_op | source)
XLA Modules:
  0.0 490.3 jit_solution(2878371439498466348)
XLA Ops:
  6.5 1.9 copy.32
  12.5 53.0 %all-gather.4.cloned.1.call-done = bf16[2048,1024]{0,1:T(8,128)(2,1)} async-done(((bf16[128,1024]{0,1:T(8,128)(2,1)}), bf16[2048,1024]{0,1:T(8,128)(2,1)}) %all-gather.4.cloned.1.call-update) | async-done | bytes 4194320 | tf_op jit(solution)/shard_map/all_gather | solution.py:35
  65.5 71.7 %while.15 = (s32[]{:T(128)}, f32[16,2048]{1,0:T(8,128)S(1)}, f32[16,2048]{1,0:T(8,128)S(1)}, f32[16,2048,64]{1,2,0:T(8,128)}, bf16[16,2048,64]{1,2,0:T(8,128)(2,...) while((s32[]{:T(128)}, f32[16,2048]{1,0:T(8,128)S(1)}, ...), condition=%wide.region_5.6_spmd.clone, body=%wide.region_2.5_spmd.clone.sunk | while | flops 70250496 | bytes 4058741 | solution.py:56
  71.2 1.8 fusion.73
  75.7 1.8 fusion.73
  80.2 1.8 fusion.73
  84.7 1.8 fusion.73
  89.2 1.8 fusion.73
  98.1 1.8 fusion.73
  102.6 1.8 fusion.73
  107.1 1.8 fusion.73
  111.6 1.8 fusion.73
  116.1 1.8 fusion.73
  120.6 1.8 fusion.73
  125.0 1.8 fusion.73
  134.0 1.8 fusion.73
  137.8 3.5 all-to-all-start.1
  142.0 7.2 %all-to-all-done.1 = f32[16,128,16]{1,2,0:T(8,128)S(1)} async-done(((f32[16,128,16]{1,2,0:T(8,128)}), f32[16,128,16]{1,2,0:T(8,128)S(1)}, u32[]{:S(2)}, u32[]{:S(2)}) %all-to-all-start.1) | async-done | bytes 131104 | tf_op jit(solution)/shard_map/all_to_all | solution.py:71
  149.2 3.5 all-to-all-start.2
  152.8 5.4 %copy.49 = f32[128,8,16,128]{3,2,1,0:T(8,128)S(1)} copy(f32[128,8,16,128]{3,1,2,0:T(8,128)} %bitcast.87) | data formatting | bytes 16777216
  158.1 5.8 %copy.38 = f32[16,128,1024]{1,2,0:T(8,128)} copy(f32[16,128,1024]{1,0,2:T(8,128)S(1)} %bitcast.86) | data formatting | bytes 16777216 | tf_op jit(solution)/shard_map/reshape;reshape | solution.py:65
  163.9 6.0 %all-to-all-start = ((f32[16,128,1024]{1,2,0:T(8,128)}), f32[16,128,1024]{1,2,0:T(8,128)}, u32[]{:S(2)}, u32[]{:S(2)}) async-start(f32[16,128,1024]{1,2,0:T(8,128)} %copy.38), calls=%async_computation | async-start | bytes 16777216 | tf_op jit(solution)/shard_map/all_to_all | solution.py:64
  170.1 150.6 %all-to-all-done = f32[16,128,1024]{1,2,0:T(8,128)} async-done(((f32[16,128,1024]{1,2,0:T(8,128)}), f32[16,128,1024]{1,2,0:T(8,128)}, u32[]{:S(2)}, u32[]{:S(2)}) %all-to-all-start) | async-done | bytes 8388640 | tf_op jit(solution)/shard_map/all_to_all | solution.py:64
  320.7 4.0 fusion.24
  324.8 2.1 fusion.49
  327.1 3.8 convolution_convert_fusion
  332.7 81.6 %all-gather.8.cloned.1.call-done = bf16[2048,1024]{1,0:T(8,128)(2,1)} async-done(((bf16[128,1024]{1,0:T(8,128)(2,1)}), bf16[2048,1024]{1,0:T(8,128)(2,1)}) %all-gather.8.cloned.1.call-update) | async-done | bytes 4194320 | tf_op jit(solution)/shard_map/all_gather | solution.py:103
  414.3 6.5 %copy.43 = bf16[2048,1024]{0,1:T(8,128)(2,1)} copy(bf16[2048,1024]{1,0:T(8,128)(2,1)} %all-gather.8.cloned.1.call-done) | data formatting | bytes 8388608 | tf_op jit(solution)/shard_map/all_gather | solution.py:103
  420.8 9.9 %fusion.50 = (f32[16,128]{1,0:T(8,128)S(1)}, f32[16,128,2048]{2,1,0:T(8,128)}) fusion(bf16[128,16,64]{0,2,1:T(8,128)(2,1)S(1)} %bitcast.95, bf16[2048,16,64]{0,2,1:T(8,128)(2,1)} %bitcast.88), kind=kOutput, calls=%fused_computation.72 | convolution fusion | flops 549455872 | bytes 21241856 | tf_op jit(solution)/shard_map/sub | solution.py:113
  430.8 35.0 %all-gather.6.cloned.1.call-done = bf16[2048,1024]{1,0:T(8,128)(2,1)} async-done(((bf16[128,1024]{1,0:T(8,128)(2,1)}), bf16[2048,1024]{1,0:T(8,128)(2,1)}) %all-gather.6.cloned.1.call-update) | async-done | bytes 4194320 | tf_op jit(solution)/shard_map/all_gather | solution.py:104
  465.7 6.5 %copy.41 = bf16[2048,1024]{0,1:T(8,128)(2,1)} copy(bf16[2048,1024]{1,0:T(8,128)(2,1)} %all-gather.6.cloned.1.call-done) | data formatting | bytes 8388608 | tf_op jit(solution)/shard_map/all_gather | solution.py:104
  472.3 10.3 %fusion.30 = bf16[16,64,128]{2,1,0:T(8,128)(2,1)S(1)} fusion(bf16[2048,16,64]{0,2,1:T(8,128)(2,1)} %bitcast.89, f32[16,128,2048]{2,1,0:T(8,128)} %get-tuple-element.131, f32[16,128]{1,0:T(8,128)S(1)} %get-tuple-element.130), kind=kOutput, calls=%fused_computation.36 | convolution fusion | flops 545390592 | bytes 21241856 | tf_op jit(solution)/shard_map/hrm,mhe->rhe/dot_general | solution.py:115
  (105 shorter events, 55.8 us)
Async XLA Ops:
  6.5 4.1 copy-start
  6.5 58.9 %all-gather.4.cloned.1.call-start = ((), (), s32[]{:S(2)}) async-start(), calls=%async_computation.3 | async-start | bytes 4456448 | tf_op jit(solution)/shard_map/all_gather | solution.py:35
  137.8 11.4 %all-to-all-start.1 = ((f32[16,128,16]{1,2,0:T(8,128)}), f32[16,128,16]{1,2,0:T(8,128)S(1)}, u32[]{:S(2)}, u32[]{:S(2)}) async-start(f32[16,128,16]{1,2,0:T(8,128)} %copy_bitcast_fusion.1), calls=%async_computation.1 | async-start | bytes 262144 | tf_op jit(solution)/shard_map/all_to_all | solution.py:71
  149.2 14.7 %all-to-all-start.2 = ((f32[16,128,16]{1,2,0:T(8,128)}), f32[16,128,16]{1,2,0:T(8,128)S(1)}, u32[]{:S(2)}, u32[]{:S(2)}) async-start(f32[16,128,16]{1,2,0:T(8,128)} %copy_bitcast_fusion), calls=%async_computation.2 | async-start | bytes 262144 | tf_op jit(solution)/shard_map/all_to_all | solution.py:78
  163.9 156.7 %all-to-all-start = ((f32[16,128,1024]{1,2,0:T(8,128)}), f32[16,128,1024]{1,2,0:T(8,128)}, u32[]{:S(2)}, u32[]{:S(2)}) async-start(f32[16,128,1024]{1,2,0:T(8,128)} %copy.38), calls=%async_computation | async-start | bytes 16777216 | tf_op jit(solution)/shard_map/all_to_all | solution.py:64
  170.0 154.8 %copy-start.3 = (bf16[128,1024]{1,0:T(8,128)(2,1)S(1)}, bf16[128,1024]{1,0:T(8,128)(2,1)}, u32[]{:S(2)}) copy-start(bf16[128,1024]{1,0:T(8,128)(2,1)} %param.12) | copy-start | bytes 786436
  170.0 244.4 %all-gather.8.cloned.1.call-start = ((), (), s32[]{:S(2)}) async-start(), calls=%async_computation.5 | async-start | bytes 4456448 | tf_op jit(solution)/shard_map/all_gather | solution.py:103
  331.8 133.9 %all-gather.6.cloned.1.call-start = ((), (), s32[]{:S(2)}) async-start(), calls=%async_computation.4 | async-start | bytes 4456448 | tf_op jit(solution)/shard_map/all_gather | solution.py:104
  472.3 10.3 %copy-start.2 = (bf16[1024,1024]{1,0:T(8,128)(2,1)S(1)}, bf16[1024,1024]{1,0:T(8,128)(2,1)}, u32[]{:S(2)}) copy-start(bf16[1024,1024]{1,0:T(8,128)(2,1)} %param.17) | copy-start | bytes 6291460
  472.3 11.5 %copy-start.1 = (bf16[512,2048]{1,0:T(8,128)(2,1)S(1)}, bf16[512,2048]{1,0:T(8,128)(2,1)}, u32[]{:S(2)}) copy-start(bf16[512,2048]{1,0:T(8,128)(2,1)} %param.14) | copy-start | bytes 6291460
Sparse Core Ops, SparseCore 0:
  9.5 55.9 all-gather.3
  331.9 82.3 all-gather.7
  416.5 49.1 all-gather.5
where the time goes:
time: 492 us; the launch traced here: 490 us
  waiting for transfers between devices  328 us (67%)
  matrix products  78.9 us (16%)
  local copies, waits for them, and re-layouts  35.4 us (7%)
  other arithmetic  20.7 us (4%)
  starting transfers between devices  13.3 us (3%)
  between operations  13.3 us (3%)
    all_to_all x1, waiting for transfers between devices, shards(): lax.all_to_all(run_acc.reshape(sources, owned_rows, feature_width), 'fram...  151 us
    all_gather x1, waiting for transfers between devices, shards(): lax.all_gather(self_key, 'frame', axis=0, tiled=True)  81.6 us
    all_gather x1, waiting for transfers between devices, shards(): piece = lax.all_gather(latent_queries, 'frame', axis=0, tiled=True)  53 us
    all_gather x1, waiting for transfers between devices, shards(): lax.all_gather(self_value, 'frame', axis=0, tiled=True)  35 us
    dot_general x16, matrix products, one_head(): jnp.dot(weights.astype(jnp.bfloat16), value_head, preferred_element_type=...  29.2 us
    dot_general x16, matrix products, one_head(): jnp.einsum('re,fe->rf', query_head, key_head, preferred_element_type=jnp....  21.1 us
    reduce_sum x16, other arithmetic, one_head(): block_total = jnp.sum(weights, axis=1)  14.3 us
    dot_general x1, matrix products, shards(): jnp.einsum('hrm,mhe->rhe', probs, every_value, preferred_element_type=jnp...  10.3 us
  transfers between devices with their start and end apart: 6, of which 5 were waited for; matrix products, arithmetic and copies ran while one was open for 7% of the time, Pallas kernels for 0%

commit v1 on v0

--- a/solution.py
+++ b/solution.py
@@ -119,6 +119,60 @@
     )
 
 
+def shards_small(frames, segment, latents, latent_queries, w_kv, w_cross_out, w_self_qkv, w_self_out):
+    width = w_kv.shape[1] // 2
+    rows = latents.shape[0]
+    scale = 1.0 / math.sqrt(HEAD_DIM)
+    first = lax.axis_index("frame") * rows
+    own_ids = (first + jnp.arange(rows, dtype=jnp.int32)) // (L // NB) + 1
+    every_frame = lax.all_gather(frames, "frame", axis=0, tiled=True)
+    every_segment = lax.all_gather(segment, "frame", axis=0, tiled=True)
+    normed = layer_norm(every_frame.astype(jnp.float32)).astype(jnp.bfloat16)
+    keyval = jnp.dot(normed, w_kv, preferred_element_type=jnp.float32).astype(jnp.bfloat16)
+    count = keyval.shape[0]
+    keys = keyval[:, :width].reshape(count, H, HEAD_DIM)
+    vals = keyval[:, width:].reshape(count, H, HEAD_DIM)
+    queries = latent_queries.reshape(rows, H, HEAD_DIM)
+    allowed = (every_segment[None, :] == own_ids[:, None])[None]
+    score = jnp.einsum("rhe,fhe->hrf", queries, keys, preferred_element_type=jnp.float32) * scale
+    score = jnp.where(allowed, score, NEG)
+    peak = jnp.max(score, axis=2, keepdims=True)
+    weights = jnp.where(allowed, jnp.exp(score - peak), 0.0)
+    total = jnp.sum(weights, axis=2)
+    summed = jnp.einsum(
+        "hrf,fhe->hre", weights.astype(jnp.bfloat16), vals, preferred_element_type=jnp.float32
+    )
+    cross = (summed / total[:, :, None]).transpose(1, 0, 2).reshape(rows, width)
+    cross = cross.astype(jnp.bfloat16)
+    mixed = latents.astype(jnp.float32) + jnp.dot(
+        cross, w_cross_out, preferred_element_type=jnp.float32
+    )
+    normed_latent = layer_norm(mixed).astype(jnp.bfloat16)
+    every_latent = lax.all_gather(normed_latent, "frame", axis=0, tiled=True)
+    self_query = jnp.dot(
+        normed_latent, w_self_qkv[:, :width], preferred_element_type=jnp.float32
+    ).astype(jnp.bfloat16)
+    self_keyval = jnp.dot(
+        every_latent, w_self_qkv[:, width:], preferred_element_type=jnp.float32
+    ).astype(jnp.bfloat16)
+    total_rows = every_latent.shape[0]
+    self_query = self_query.reshape(rows, H, HEAD_DIM)
+    self_key = self_keyval[:, :width].reshape(total_rows, H, HEAD_DIM)
+    self_value = self_keyval[:, width:].reshape(total_rows, H, HEAD_DIM)
+    score = (
+        jnp.einsum("rhe,mhe->hrm", self_query, self_key, preferred_element_type=jnp.float32)
+        * scale
+    )
+    peak = jnp.max(score, axis=2, keepdims=True)
+    expo = jnp.exp(score - peak)
+    probs = (expo / jnp.sum(expo, axis=2, keepdims=True)).astype(jnp.bfloat16)
+    attended = jnp.einsum("hrm,mhe->rhe", probs, self_value, preferred_element_type=jnp.float32)
+    attended = attended.reshape(rows, width).astype(jnp.bfloat16)
+    return (mixed + jnp.dot(attended, w_self_out, preferred_element_type=jnp.float32)).astype(
+        jnp.bfloat16
+    )
+
+
 def solution(mesh):
     placed = (
         P(("rep", "frame"), None),
@@ -130,6 +184,7 @@
         P(),
         P(),
     )
+    body = shards_small if mesh.shape["frame"] <= 16 else shards
     return jax.shard_map(
-        shards, mesh=mesh, in_specs=placed, out_specs=P(("rep", "frame"), None), check_vma=False
+        body, mesh=mesh, in_specs=placed, out_specs=P(("rep", "frame"), None), check_vma=False
     )

time: 492 us -> 181 us (0.37)
  waiting for transfers between devices: 328 us -> 69.6 us
  local copies, waits for them, and re-layouts: 35.4 us -> 8.62 us
  blocking collectives: 0 us -> 23.1 us
  matrix products: 78.9 us -> 59.5 us
  other arithmetic: 20.7 us -> 5.99 us
  starting transfers between devices: 13.3 us -> 0.04 us
    all_to_all x3 -> x0, waiting for transfers between devices: 158 us -> none  [the longest x1 151 us: shards(): lax.all_to_all(run_acc.reshape(sources, owned_rows, feature_width), 'fram...]
    all_gather x3 -> x2, waiting for transfers between devices: 170 us -> 68.9 us  [the longest x1 47.2 us: shards_small(): every_latent = lax.all_gather(normed_latent, 'frame', axis=0, tiled=True)]
    dot_general x37 -> x7, matrix products: 69 us -> 37.6 us  [the longest x1 12 us: shards_small(): jnp.dot(every_latent, w_self_qkv[:, width:], preferred_element_type=jnp.f...]
    all_gather x0 -> x1, blocking collectives: none -> 23.1 us  [shards_small(): every_segment = lax.all_gather(segment, 'frame', axis=0, tiled=True)]
    reduce_sum x18 -> x0, other arithmetic: 18.3 us -> none  [the longest x16 14.3 us: one_head(): block_total = jnp.sum(weights, axis=1)]
    all_to_all x3 -> x0, starting transfers between devices: 13 us -> none  [the longest x1 6.02 us: shards(): lax.all_to_all(run_acc.reshape(sources, owned_rows, feature_width), 'fram...]
    all_gather x2 -> x0, local copies, waits for them, and re-layouts: 13 us -> none  [the longest x1 6.51 us: shards(): lax.all_gather(self_value, 'frame', axis=0, tiled=True)]
    sub x1 -> x2, matrix products: 9.92 us -> 21.9 us  [the longest x1 12.1 us: shards_small(): weights = jnp.where(allowed, jnp.exp(score - peak), 0.0)]
  transfers between devices with their start and end apart: 6 -> 2, of which waited for: 5 -> 2; matrix products, arithmetic and copies ran while one was open for 7% -> 2% of each run, Pallas kernels for 0% -> 0%
where the time goes in v1:
time: 181 us; the launch traced here: 180 us
  waiting for transfers between devices  69.6 us (38%)
  matrix products  59.5 us (33%)
  blocking collectives  23.1 us (13%)
  between operations  13.5 us (7%)
  local copies, waits for them, and re-layouts  8.62 us (5%)
  other arithmetic  5.99 us (3%)
    all_gather x1, waiting for transfers between devices, shards_small(): every_latent = lax.all_gather(normed_latent, 'frame', axis=0, tiled=True)  47.2 us
    all_gather x1, blocking collectives, shards_small(): every_segment = lax.all_gather(segment, 'frame', axis=0, tiled=True)  23.1 us
    all_gather x1, waiting for transfers between devices, shards_small(): every_frame = lax.all_gather(frames, 'frame', axis=0, tiled=True)  21.7 us
    sub x1, matrix products, shards_small(): weights = jnp.where(allowed, jnp.exp(score - peak), 0.0)  12.1 us
    dot_general x1, matrix products, shards_small(): jnp.dot(every_latent, w_self_qkv[:, width:], preferred_element_type=jnp.f...  12 us
    dot_general x1, matrix products, shards_small(): jnp.einsum('hrm,mhe->rhe', probs, self_value, preferred_element_type=jnp....  10.3 us
    sub x1, matrix products, shards_small(): expo = jnp.exp(score - peak)  9.82 us
    dot_general x1, matrix products, shards_small(): jnp.einsum('hrf,fhe->hre', weights.astype(jnp.bfloat16), vals, preferred_...  6.36 us
  transfers between devices with their start and end apart: 2, of which 2 were waited for; matrix products, arithmetic and copies ran while one was open for 2% of the time, Pallas kernels for 0%

profile of v1, /device:TPU:0, one launch (start us, length us, event | category | flops | bytes accessed | tf_op | source)
XLA Modules:
  0.0 180.5 jit_solution(12245274209574374046)
XLA Ops:
  6.5 0.0 copy-start
  6.5 0.0 all-gather.4.cloned.1.call-start
  6.5 0.7 all-gather.4.cloned.1.call-update
  7.3 0.0 all-gather.6.cloned.1.call-start
  7.3 1.1 copy.15
  8.4 23.1 %all-gather = s32[16,1,128]{2,1,0:T(1,128)S(1)} all-gather(s32[1,1,128]{2,1,0:T(1,128)} %bitcast.58), channel_id=1, replica_groups=mesh['rep'=2,'frame'=16] {'frame'}, dimensions={0}, use_global_device_ids=true | all-gather | bytes 8704 | tf_op jit(solution)/shard_map/all_gather | solution.py:129
  31.6 0.3 broadcast_compare_fusion
  31.9 21.7 %all-gather.4.cloned.1.call-done = bf16[2048,512]{1,0:T(8,128)(2,1)} async-done(((bf16[128,512]{1,0:T(8,128)(2,1)}), bf16[2048,512]{1,0:T(8,128)(2,1)}) %all-gather.4.cloned.1.call-update) | async-done | bytes 2097168 | tf_op jit(solution)/shard_map/all_gather | solution.py:128
  53.7 2.1 %convert_reduce_fusion = f32[2048]{0:T(1024)S(1)} fusion(bf16[2048,512]{1,0:T(8,128)(2,1)} %all-gather.4.cloned.1.call-done), kind=kLoop, calls=%fused_computation.19 | loop fusion | flops 2095104 | bytes 2105344 | tf_op jit(solution)/shard_map/reduce_sum | solution.py:18
  55.8 2.5 %fusion.15 = f32[2048]{0:T(1024)S(1)} fusion(bf16[2048,512]{1,0:T(8,128)(2,1)} %all-gather.4.cloned.1.call-done, f32[2048]{0:T(1024)S(1)} %broadcast_multiply_fusion), kind=kLoop, calls=%fused_computation.22 | loop fusion | flops 4192256 | bytes 2113536 | tf_op jit(solution)/shard_map/reduce_sum | solution.py:19
  58.3 0.0 copy-done
  58.3 0.0 copy-done.2
  58.3 5.1 %convolution_convert_fusion.1 = bf16[2048,2048]{0,1:T(8,128)(2,1)S(1)} fusion(bf16[512,2048]{1,0:T(8,128)(2,1)S(1)} %copy-done, bf16[2048,512]{1,0:T(8,128)(2,1)S(1)} %copy-done.2, f32[2048]{0:T(1024)S(1)} %add_rsqrt_fusion, f32[2048]{0:T(1024)S(1)} %broadcast_multiply_fusion), kind=kOutput, calls=%fused_computation.17 | convolution fusion | flops 4303355904 | bytes 12599296 | tf_op jit(solution)/shard_map/dot_general | solution.py:131
  63.4 3.7 %fusion.46 = (bf16[2048,1024]{0,1:T(8,128)(2,1)}, bf16[2048,1024]{0,1:T(8,128)(2,1)}) fusion(bf16[2048,2048]{0,1:T(8,128)(2,1)S(1)} %convolution_convert_fusion.1), kind=kLoop, calls=%fused_computation.55 | loop fusion | bytes 16777216 | tf_op jit(solution)/shard_map/slice | solution.py:133
  67.2 12.1 %fusion.47 = (f32[16,128]{1,0:T(8,128)S(1)}, bf16[16,128,2048]{1,2,0:T(8,128)(2,1)}) fusion(pred[128,2048]{0,1:T(8,128)(4,1)S(1)} %broadcast_compare_fusion, bf16[2048,16,64]{0,2,1:T(8,128)(2,1)} %bitcast.50, bf16[128,16,64]{0,2,1:T(8,128)(2,1)S(1)} %bitcast.54), kind=kOutput, calls=%fused_computation.56 | convolution fusion | flops 562038784 | bytes 13115392 | tf_op jit(solution)/shard_map/sub | solution.py:140
  79.3 6.4 %fusion.31 = bf16[128,16,64]{0,2,1:T(8,128)(2,1)S(1)} fusion(bf16[2048,16,64]{0,2,1:T(8,128)(2,1)} %bitcast.48, bf16[16,128,2048]{1,2,0:T(8,128)(2,1)} %get-tuple-element.10, f32[128,16]{0,1:T(8,128)S(1)} %bitcast.56), kind=kOutput, calls=%fused_computation.34 | convolution fusion | flops 537133056 | bytes 12853248 | tf_op jit(solution)/shard_map/hrf,fhe->hre/dot_general | solution.py:142
  85.6 0.0 copy-done.4
  85.6 0.0 copy-done.5
  85.7 0.6 fusion.48
  86.2 0.2 multiply_reduce_fusion.1
  86.4 0.8 multiply_convert_fusion
  87.3 0.0 all-gather.6.cloned.1.call-update
  87.3 2.1 %fusion.34 = bf16[128,1024]{1,0:T(8,128)(2,1)S(1)} fusion(bf16[128,1024]{1,0:T(8,128)(2,1)} %multiply_convert_fusion, bf16[1024,3072]{1,0:T(8,128)(2,1)} %param.14), kind=kOutput, calls=%fused_computation.35 | convolution fusion | flops 268566528 | bytes 2621440 | tf_op jit(solution)/shard_map/dot_general | solution.py:152
  89.4 0.2 copy.17
  89.6 47.2 %all-gather.6.cloned.1.call-done = bf16[2048,1024]{1,0:T(8,128)(2,1)} async-done(((bf16[128,1024]{1,0:T(8,128)(2,1)}), bf16[2048,1024]{1,0:T(8,128)(2,1)}) %all-gather.6.cloned.1.call-update) | async-done | bytes 4194320 | tf_op jit(solution)/shard_map/all_gather | solution.py:151
  136.8 12.0 %convolution_convert_fusion = bf16[2048,2048]{0,1:T(8,128)(2,1)S(1)} fusion(bf16[2048,1024]{1,0:T(8,128)(2,1)} %all-gather.6.cloned.1.call-done, bf16[1024,3072]{1,0:T(8,128)(2,1)} %param.14), kind=kOutput, calls=%fused_computation.16 | convolution fusion | flops 8594128896 | bytes 16777216 | tf_op jit(solution)/shard_map/dot_general | solution.py:155
  148.8 3.6 %fusion.45 = (bf16[2048,1024]{0,1:T(8,128)(2,1)}, bf16[2048,1024]{0,1:T(8,128)(2,1)}) fusion(bf16[2048,2048]{0,1:T(8,128)(2,1)S(1)} %convolution_convert_fusion), kind=kLoop, calls=%fused_computation.54 | loop fusion | bytes 16777216 | tf_op jit(solution)/shard_map/slice | solution.py:160
  152.3 9.8 %fusion.49 = (f32[16,128]{1,0:T(8,128)S(1)}, f32[16,128,2048]{2,1,0:T(8,128)}) fusion(bf16[128,16,64]{0,2,1:T(8,128)(2,1)S(1)} %bitcast.55, bf16[2048,16,64]{0,2,1:T(8,128)(2,1)} %bitcast.51), kind=kOutput, calls=%fused_computation.58 | convolution fusion | flops 549455872 | bytes 21241856 | tf_op jit(solution)/shard_map/sub | solution.py:167
  162.2 10.3 %fusion.38 = bf16[16,64,128]{2,1,0:T(8,128)(2,1)S(1)} fusion(bf16[2048,16,64]{0,2,1:T(8,128)(2,1)} %bitcast.49, f32[16,128,2048]{2,1,0:T(8,128)} %get-tuple-element.14, f32[16,128]{1,0:T(8,128)S(1)} %get-tuple-element.13), kind=kOutput, calls=%fused_computation.37 | convolution fusion | flops 545390592 | bytes 21241856 | tf_op jit(solution)/shard_map/hrm,mhe->rhe/dot_general | solution.py:169
  172.4 0.0 copy-done.3
  172.5 1.2 fusion.37
  173.6 0.0 copy-done.1
  (10 shorter events, 0.0 us)
Async XLA Ops:
  6.5 51.7 %copy-start = (bf16[512,2048]{1,0:T(8,128)(2,1)S(1)}, bf16[512,2048]{1,0:T(8,128)(2,1)}, u32[]{:S(2)}) copy-start(bf16[512,2048]{1,0:T(8,128)(2,1)} %param.12) | copy-start | bytes 6291460
  6.5 47.1 %all-gather.4.cloned.1.call-start = ((), (), s32[]{:S(2)}) async-start(), calls=%async_computation | async-start | bytes 2228224 | tf_op jit(solution)/shard_map/all_gather | solution.py:128
  7.3 129.5 %all-gather.6.cloned.1.call-start = ((), (), s32[]{:S(2)}) async-start(), calls=%async_computation.1 | async-start | bytes 4456448 | tf_op jit(solution)/shard_map/all_gather | solution.py:151
  53.7 4.6 %copy-start.2 = (bf16[2048,512]{1,0:T(8,128)(2,1)S(1)}, bf16[2048,512]{1,0:T(8,128)(2,1)}, u32[]{:S(2)}) copy-start(bf16[2048,512]{1,0:T(8,128)(2,1)} %all-gather.4.cloned.1.call-done) | copy-start | bytes 6291460
  79.3 6.4 %copy-start.4 = (bf16[1024,1024]{1,0:T(8,128)(2,1)S(1)}, bf16[1024,1024]{1,0:T(8,128)(2,1)}, u32[]{:S(2)}) copy-start(bf16[1024,1024]{1,0:T(8,128)(2,1)} %param.13) | copy-start | bytes 6291460
  79.3 6.4 %copy-start.5 = (bf16[128,1024]{1,0:T(8,128)(2,1)S(1)}, bf16[128,1024]{1,0:T(8,128)(2,1)}, u32[]{:S(2)}) copy-start(bf16[128,1024]{1,0:T(8,128)(2,1)} %param.10) | copy-start | bytes 786436
  162.2 10.3 %copy-start.3 = (bf16[1024,1024]{1,0:T(8,128)(2,1)S(1)}, bf16[1024,1024]{1,0:T(8,128)(2,1)}, u32[]{:S(2)}) copy-start(bf16[1024,1024]{1,0:T(8,128)(2,1)} %param.15) | copy-start | bytes 6291460
  162.2 11.5 %copy-start.1 = (bf16[512,2048]{1,0:T(8,128)(2,1)S(1)}, bf16[512,2048]{1,0:T(8,128)(2,1)}, u32[]{:S(2)}) copy-start(bf16[512,2048]{1,0:T(8,128)(2,1)} %param.12) | copy-start | bytes 6291460
Sparse Core Ops, SparseCore 0:
  9.5 44.0 all-gather.3
  87.4 49.3 all-gather.5

commit v2 on v0

--- a/solution.py
+++ b/solution.py
@@ -3,6 +3,8 @@
 import jax
 import jax.numpy as jnp
 from jax import lax
+from jax.experimental import pallas as pl
+from jax.experimental.pallas import tpu as pltpu
 from jax.sharding import PartitionSpec as P
 
 H = 16
@@ -119,6 +121,458 @@
     )
 
 
+NX = 2
+NZ = 4
+PAIRS = H // 2
+MESH = pl.DeviceIdType.MESH
+
+
+def pick(index, values):
+    chosen = values[0]
+    for position in range(1, len(values)):
+        chosen = jnp.where(index == position, values[position], chosen)
+    return chosen
+
+
+class Place:
+    def __init__(self):
+        self.me = lax.axis_index("frame")
+        self.z = self.me // 4
+        self.x = lax.rem(self.me // 2, 2)
+        self.core = lax.rem(self.me, 2)
+        self.sibling = self.index(self.z, self.x, 1 - self.core)
+        self.across = self.index(self.z, 1 - self.x, self.core)
+        self.above = self.me + 4
+        self.below = self.me - 4
+        self.has_above = self.z < NZ - 1
+        self.has_below = self.z > 0
+        self.order = [
+            self.z,
+            pick(self.z, (1, 2, 1, 2)),
+            pick(self.z, (2, 0, 3, 1)),
+            pick(self.z, (3, 3, 0, 0)),
+        ]
+
+    def index(self, z, x, core):
+        return z * 4 + x * 2 + core
+
+
+def greet(targets):
+    barrier = pltpu.get_barrier_semaphore()
+    for target, there in targets:
+        if there is None:
+            pl.semaphore_signal(barrier, inc=1, device_id={"frame": target}, device_id_type=MESH)
+        else:
+
+            @pl.when(there)
+            def _():
+                pl.semaphore_signal(
+                    barrier, inc=1, device_id={"frame": target}, device_id_type=MESH
+                )
+
+    return barrier
+
+
+STEPS = (("z", 0), ("z", 1), ("x", 0), ("z", 2), ("x", 1), ("z", 3), ("x", 2), ("x", 3))
+
+
+def push(src, dst, send, recv, target):
+    return pltpu.make_async_remote_copy(
+        src_ref=src,
+        dst_ref=dst,
+        send_sem=send,
+        recv_sem=recv,
+        device_id={"frame": target},
+        device_id_type=MESH,
+    )
+
+
+def relays(place, k, slot, src, gathered, send_up, send_down, send_x, recv):
+    source_z = place.order[k]
+    up = jnp.logical_and(source_z <= place.z, place.has_above)
+    down = jnp.logical_and(source_z >= place.z, place.has_below)
+    to = gathered.at[slot]
+    return [
+        (push(src, to, send_up.at[k], recv.at[slot], place.above), up),
+        (push(src, to, send_down.at[k], recv.at[slot], place.below), down),
+        (push(src, to, send_x.at[k], recv.at[slot], place.across), None),
+    ]
+
+
+def start_all(copies):
+    for copy, there in copies:
+        if there is None:
+            copy.start()
+        else:
+            pl.when(there)(copy.start)
+
+
+def wait_sent(copies):
+    for copy, there in copies:
+        if there is None:
+            copy.wait_send()
+        else:
+            pl.when(there)(copy.wait_send)
+
+
+def gather_kernel(
+    frames, seg, every, ids, seg8, send_up, send_down, send_x, send_core, recv, seg_send, seg_recv, local
+):
+    place = Place()
+    me = place.me
+    barrier = greet([(lax.rem(me + d, 16), None) for d in range(1, 16)])
+    seg8[...] = jnp.broadcast_to(seg[...], seg8.shape)
+    own = pltpu.make_async_copy(frames, every.at[me], local.at[0])
+    own.start()
+    own_ids = pltpu.make_async_copy(seg8, ids.at[me], local.at[1])
+    own_ids.start()
+    pl.semaphore_wait(barrier, 15)
+    sent = []
+    for kind, k in STEPS:
+        x = place.x if kind == "z" else 1 - place.x
+        slot = place.index(place.order[k], x, place.core)
+        first = kind == "z" and k == 0
+        src = frames if first else every.at[slot]
+        if not first:
+            push(src, every.at[slot], send_core.at[0], recv.at[slot], place.sibling).wait_recv()
+        copies = []
+        if kind == "z":
+            copies = relays(place, k, slot, src, every, send_up, send_down, send_x, recv)
+        number = k + (0 if kind == "z" else 4)
+        copies.append(
+            (push(src, every.at[slot], send_core.at[number], recv.at[slot], place.sibling), None)
+        )
+        start_all(copies)
+        sent += copies
+        if first:
+            for d in range(1, 16):
+                copy = push(
+                    seg8, ids.at[me], seg_send.at[d], seg_recv.at[d], lax.rem(me + d, 16)
+                )
+                copy.start()
+                sent.append((copy, None))
+    for kind, k in STEPS:
+        x = place.x if kind == "z" else 1 - place.x
+        slot = place.index(place.order[k], x, 1 - place.core)
+        push(
+            every.at[slot], every.at[slot], send_core.at[0], recv.at[slot], place.sibling
+        ).wait_recv()
+    for d in range(1, 16):
+        source = lax.rem(me - d + 16, 16)
+        push(seg8, ids.at[source], seg_send.at[d], seg_recv.at[d], source).wait_recv()
+    wait_sent(sent)
+    own.wait()
+    own_ids.wait()
+
+
+def gather_frames(frames, segment):
+    dma = pltpu.SemaphoreType.DMA
+    rows, channels = frames.shape
+    return pl.pallas_call(
+        gather_kernel,
+        out_shape=(
+            jax.ShapeDtypeStruct((16, rows, channels), frames.dtype),
+            jax.ShapeDtypeStruct((16, 8, rows), jnp.int32),
+        ),
+        in_specs=[pl.BlockSpec(memory_space=pl.ANY), pl.BlockSpec(memory_space=pltpu.VMEM)],
+        out_specs=[pl.BlockSpec(memory_space=pl.ANY)] * 2,
+        scratch_shapes=[
+            pltpu.VMEM((8, rows), jnp.int32),
+            dma((4,)),
+            dma((4,)),
+            dma((4,)),
+            dma((8,)),
+            dma((16,)),
+            dma((16,)),
+            dma((16,)),
+            dma((2,)),
+        ],
+        compiler_params=pltpu.CompilerParams(
+            collective_id=0, has_side_effects=True, vmem_limit_bytes=4 * 2**20
+        ),
+        name="gather_frames",
+    )(frames, segment.reshape(1, rows))
+
+
+def split_pair(pair):
+    lane = lax.broadcasted_iota(jnp.int32, pair.shape, 1)
+    zero = jnp.zeros_like(pair)
+    return jnp.concatenate(
+        [jnp.where(lane < HEAD_DIM, pair, zero), jnp.where(lane < HEAD_DIM, zero, pair)], axis=0
+    )
+
+
+def clear(peak, total, acc):
+    peak[...] = jnp.full(peak.shape, -jnp.inf, jnp.float32)
+    total[...] = jnp.zeros(total.shape, jnp.float32)
+    acc[...] = jnp.zeros(acc.shape, jnp.float32)
+
+
+def attend(p, query, key, value, peak, total, acc, keep=None):
+    score = lax.dot_general(
+        query, key, (((1,), (1,)), ((), ())), preferred_element_type=jnp.float32
+    )
+    if keep is not None:
+        column = lax.broadcasted_iota(jnp.int32, score.shape, 1)
+        score = jnp.where(column < keep, score, -jnp.inf)
+    before = peak[p]
+    now = jnp.maximum(before, jnp.max(score, axis=1, keepdims=True))
+    half = now.shape[1]
+    left = jnp.exp(score[:, :half] - now)
+    right = jnp.exp(score[:, half:] - now)
+    fade = jnp.exp(before - now)
+    peak[p] = now
+    total[p] = total[p] * fade + (left + right)
+    weights = jnp.concatenate([left.astype(jnp.bfloat16), right.astype(jnp.bfloat16)], axis=1)
+    acc[p] = acc[p] * fade + jnp.dot(weights, value, preferred_element_type=jnp.float32)
+
+
+def join_pair(p, total, acc):
+    rows = acc.shape[1] // 2
+    result = acc[p] / jnp.sum(total[p], axis=1, keepdims=True)
+    lane = lax.broadcasted_iota(jnp.int32, (rows, acc.shape[2]), 1)
+    return jnp.where(lane < HEAD_DIM, result[:rows], result[rows:]).astype(jnp.bfloat16)
+
+
+def pair_columns(p):
+    return pl.ds(pl.multiple_of(p * 128, 128), 128)
+
+
+def cross_kernel(
+    ids, every, queries, latents, w_kv, w_out, mixed, normed, block, keyval, query, peak, total,
+    acc, cross, chosen, sems
+):
+    wanted = lax.axis_index("frame") // 2 + 1
+    width = queries.shape[1]
+    scale = 1.0 / math.sqrt(HEAD_DIM)
+
+    def look(r, count):
+        chosen[count] = r
+        return count + jnp.where(ids[r // 2, 0, lax.rem(r, 2) * 64] == wanted, 1, 0)
+
+    count = lax.fori_loop(0, 32, look, jnp.int32(0))
+    block[...] = jnp.zeros_like(block)
+
+    def fetch(group, j):
+        run = chosen[group * 4 + j]
+        return pltpu.make_async_copy(
+            every.at[run // 2, pl.ds(pl.multiple_of(lax.rem(run, 2) * 64, 64), 64)],
+            block.at[pl.ds(j * 64, 64)],
+            sems.at[j],
+        )
+
+    def fetch_all(group):
+        for j in range(4):
+
+            @pl.when(group * 4 + j < count)
+            def _():
+                fetch(group, j).start()
+
+    fetch_all(0)
+    for p in range(PAIRS):
+        query[p] = split_pair(queries[:, p * 128 : p * 128 + 128] * scale)
+    clear(peak, total, acc)
+
+    @pl.loop(0, (count + 3) // 4)
+    def _(group):
+        for j in range(4):
+
+            @pl.when(group * 4 + j < count)
+            def _():
+                fetch(group, j).wait()
+
+        ready = layer_norm(block[...].astype(jnp.float32)).astype(jnp.bfloat16)
+
+        @pl.loop(0, 4)
+        def _(j):
+            columns = pl.ds(pl.multiple_of(j * 512, 512), 512)
+            keyval[:, columns] = jnp.dot(
+                ready, w_kv[:, columns], preferred_element_type=jnp.float32
+            ).astype(jnp.bfloat16)
+
+        fetch_all(group + 1)
+        keep = (count - group * 4) * 64
+
+        @pl.loop(0, PAIRS, unroll=2)
+        def _(p):
+            attend(
+                p, query[p], keyval[:, pair_columns(p)], keyval[:, pair_columns(p + PAIRS)],
+                peak, total, acc, keep,
+            )
+
+    for p in range(PAIRS):
+        cross[:, p * 128 : p * 128 + 128] = join_pair(p, total, acc)
+    whole = latents[...].astype(jnp.float32) + jnp.dot(
+        cross[...], w_out[...], preferred_element_type=jnp.float32
+    )
+    mixed[...] = whole
+    normed[...] = layer_norm(whole).astype(jnp.bfloat16)
+
+
+def cross_attend(ids, every, queries, latents, w_kv, w_out):
+    rows, width = latents.shape
+    vmem = pl.BlockSpec(memory_space=pltpu.VMEM)
+    return pl.pallas_call(
+        cross_kernel,
+        out_shape=(
+            jax.ShapeDtypeStruct((rows, width), jnp.float32),
+            jax.ShapeDtypeStruct((rows, width), jnp.bfloat16),
+        ),
+        in_specs=[
+            pl.BlockSpec(memory_space=pltpu.SMEM),
+            pl.BlockSpec(memory_space=pl.ANY),
+            vmem,
+            vmem,
+            vmem,
+            vmem,
+        ],
+        out_specs=[vmem, vmem],
+        scratch_shapes=[
+            pltpu.VMEM((256, every.shape[2]), jnp.bfloat16),
+            pltpu.VMEM((256, 2 * width), jnp.bfloat16),
+            pltpu.VMEM((PAIRS, 2 * rows, 128), jnp.bfloat16),
+            pltpu.VMEM((PAIRS, 2 * rows, 128), jnp.float32),
+            pltpu.VMEM((PAIRS, 2 * rows, 128), jnp.float32),
+            pltpu.VMEM((PAIRS, 2 * rows, 128), jnp.float32),
+            pltpu.VMEM((rows, width), jnp.bfloat16),
+            pltpu.SMEM((64,), jnp.int32),
+            pltpu.SemaphoreType.DMA((4,)),
+        ],
+        compiler_params=pltpu.CompilerParams(vmem_limit_bytes=24 * 2**20),
+        name="cross_attend",
+    )(ids, every, queries, latents, w_kv, w_out)
+
+
+def self_kernel(
+    normed, mixed, w_qkv, w_out, out, gathered, keyval, weights, weights_out, query, peak, total,
+    acc, joined, send_up, send_down, send_x, send_core, recv, recv_core, local
+):
+    place = Place()
+    me = place.me
+    rows, width = normed.shape
+    scale = 1.0 / math.sqrt(HEAD_DIM)
+    barrier = greet(
+        [
+            (place.sibling, None),
+            (place.across, None),
+            (place.above, place.has_above),
+            (place.below, place.has_below),
+        ]
+    )
+    load = pltpu.make_async_copy(w_qkv, weights, local.at[0])
+    load.start()
+    load_out = pltpu.make_async_copy(w_out, weights_out, local.at[1])
+    load_out.start()
+    pl.semaphore_wait(
+        barrier,
+        2 + jnp.where(place.has_above, 1, 0) + jnp.where(place.has_below, 1, 0),
+    )
+    clear(peak, total, acc)
+    sent = []
+
+    def take(step):
+        kind, k = STEPS[step]
+        x = place.x if kind == "z" else 1 - place.x
+        slot = place.index(place.order[k], x, place.core)
+        chip = place.order[k] * 2 + x
+        src = normed if step == 0 else gathered.at[slot]
+        if step > 0:
+            push(src, gathered.at[slot], send_x.at[0], recv.at[slot], place.across).wait_recv()
+        if kind == "z":
+            copies = relays(place, k, slot, src, gathered, send_up, send_down, send_x, recv)
+            start_all(copies)
+            sent.extend(copies)
+        if step == 0:
+            load.wait()
+
+            @pl.loop(0, PAIRS // 2)
+            def _(j):
+                columns = pl.ds(pl.multiple_of(j * 256, 256), 256)
+                part = jnp.dot(normed[...], weights[:, columns], preferred_element_type=jnp.float32)
+                part = part.astype(jnp.bfloat16) * scale
+                query[2 * j] = split_pair(part[:, :128])
+                query[2 * j + 1] = split_pair(part[:, 128:])
+
+        @pl.loop(0, 4)
+        def _(j):
+            columns = pl.ds(pl.multiple_of(j * 512, 512), 512)
+            wide = pl.ds(pl.multiple_of(width + j * 512, 512), 512)
+            keyval[chip, place.core, :, columns] = jnp.dot(
+                src[...], weights[:, wide], preferred_element_type=jnp.float32
+            ).astype(jnp.bfloat16)
+
+        ours = keyval.at[chip, place.core]
+        copy = push(ours, ours, send_core.at[step], recv_core.at[step], place.sibling)
+        copy.start()
+        sent.append((copy, None))
+        return chip
+
+    def use(step, chip):
+        theirs = keyval.at[chip, 1 - place.core]
+        push(theirs, theirs, send_core.at[step], recv_core.at[step], place.sibling).wait_recv()
+
+        @pl.loop(0, PAIRS, unroll=2)
+        def _(p):
+            key = keyval[chip, :, :, pair_columns(p)].reshape(2 * rows, 128)
+            value = keyval[chip, :, :, pair_columns(p + PAIRS)].reshape(2 * rows, 128)
+            attend(p, query[p], key, value, peak, total, acc)
+
+    chip = take(0)
+    for step in range(1, len(STEPS)):
+        later = take(step)
+        use(step - 1, chip)
+        chip = later
+    use(len(STEPS) - 1, chip)
+    for p in range(PAIRS):
+        joined[:, p * 128 : p * 128 + 128] = join_pair(p, total, acc)
+    load_out.wait()
+    out[...] = (
+        mixed[...] + jnp.dot(joined[...], weights_out[...], preferred_element_type=jnp.float32)
+    ).astype(jnp.bfloat16)
+    wait_sent(sent)
+
+
+def self_attend(normed, mixed, w_qkv, w_out):
+    rows, width = normed.shape
+    dma = pltpu.SemaphoreType.DMA
+    vmem = pl.BlockSpec(memory_space=pltpu.VMEM)
+    anywhere = pl.BlockSpec(memory_space=pl.ANY)
+    return pl.pallas_call(
+        self_kernel,
+        out_shape=jax.ShapeDtypeStruct((rows, width), jnp.bfloat16),
+        in_specs=[vmem, vmem, anywhere, anywhere],
+        out_specs=vmem,
+        scratch_shapes=[
+            pltpu.VMEM((16, rows, width), jnp.bfloat16),
+            pltpu.VMEM((8, 2, rows, 2 * width), jnp.bfloat16),
+            pltpu.VMEM(w_qkv.shape, jnp.bfloat16),
+            pltpu.VMEM(w_out.shape, jnp.bfloat16),
+            pltpu.VMEM((PAIRS, 2 * rows, 128), jnp.bfloat16),
+            pltpu.VMEM((PAIRS, 2 * rows, 128), jnp.float32),
+            pltpu.VMEM((PAIRS, 2 * rows, 128), jnp.float32),
+            pltpu.VMEM((PAIRS, 2 * rows, 128), jnp.float32),
+            pltpu.VMEM((rows, width), jnp.bfloat16),
+            dma((4,)),
+            dma((4,)),
+            dma((4,)),
+            dma((8,)),
+            dma((16,)),
+            dma((8,)),
+            dma((2,)),
+        ],
+        compiler_params=pltpu.CompilerParams(
+            collective_id=1, has_side_effects=True, vmem_limit_bytes=40 * 2**20
+        ),
+        name="self_attend",
+    )(normed, mixed, w_qkv, w_out)
+
+
+def shards_small(frames, segment, latents, latent_queries, w_kv, w_cross_out, w_self_qkv, w_self_out):
+    every, ids = gather_frames(frames, segment)
+    mixed, normed = cross_attend(ids, every, latent_queries, latents, w_kv, w_cross_out)
+    return self_attend(normed, mixed, w_self_qkv, w_self_out)
+
+
 def solution(mesh):
     placed = (
         P(("rep", "frame"), None),
@@ -130,6 +584,7 @@
         P(),
         P(),
     )
+    body = shards_small if mesh.shape["frame"] == 2 * NX * NZ else shards
     return jax.shard_map(
-        shards, mesh=mesh, in_specs=placed, out_specs=P(("rep", "frame"), None), check_vma=False
-    )
+        body, mesh=mesh, in_specs=placed, out_specs=P(("rep", "frame"), None), check_vma=False
+    )

time: 492 us -> 94.9 us (0.19)
  waiting for transfers between devices: 328 us -> 0 us
  Pallas kernels: 0 us -> 86.8 us
  matrix products: 78.9 us -> 0 us
  local copies, waits for them, and re-layouts: 35.4 us -> 8.93 us
  other arithmetic: 20.7 us -> 0 us
  starting transfers between devices: 13.3 us -> 0 us
  between operations: 13.3 us -> 0.06 us
    all_gather x3 -> x0, waiting for transfers between devices: 170 us -> none  [the longest x1 81.6 us: shards(): lax.all_gather(self_key, 'frame', axis=0, tiled=True)]
    all_to_all x3 -> x0, waiting for transfers between devices: 158 us -> none  [the longest x1 151 us: shards(): lax.all_to_all(run_acc.reshape(sources, owned_rows, feature_width), 'fram...]
    pallas_call x0 -> x3, Pallas kernels: none -> 86.8 us  [the longest x1 53.3 us: self_attend(): pl.pallas_call(self_kernel, out_shape=jax.ShapeDtypeStruct((rows, width),...]
    dot_general x37 -> x0, matrix products: 69 us -> none  [the longest x16 29.2 us: one_head(): jnp.dot(weights.astype(jnp.bfloat16), value_head, preferred_element_type=...]
    reduce_sum x21 -> x0, other arithmetic: 20.6 us -> none  [the longest x16 14.3 us: one_head(): block_total = jnp.sum(weights, axis=1)]
    all_to_all x3 -> x0, starting transfers between devices: 13 us -> none  [the longest x1 6.02 us: shards(): lax.all_to_all(run_acc.reshape(sources, owned_rows, feature_width), 'fram...]
    all_gather x2 -> x0, local copies, waits for them, and re-layouts: 13 us -> none  [the longest x1 6.51 us: shards(): lax.all_gather(self_value, 'frame', axis=0, tiled=True)]
    sub x1 -> x0, matrix products: 9.92 us -> none  [shards(): expo = jnp.exp(score - peak)]
  transfers between devices with their start and end apart: 6 -> 0, of which waited for: 5 -> 0; matrix products, arithmetic and copies ran while one was open for 7% -> 0% of each run, Pallas kernels for 0% -> 0%
where the time goes in v2:
time: 94.9 us; the launch traced here: 95.8 us
  Pallas kernels  86.8 us (91%)
  local copies, waits for them, and re-layouts  8.93 us (9%)
    pallas_call x1, Pallas kernels, self_attend(): pl.pallas_call(self_kernel, out_shape=jax.ShapeDtypeStruct((rows, width),...  53.3 us
    pallas_call x1, Pallas kernels, gather_frames(): pl.pallas_call(gather_kernel, out_shape=(jax.ShapeDtypeStruct((16, rows,...  25.8 us
    unnamed x17, local copies, waits for them, and re-layouts  8.93 us
    pallas_call x1, Pallas kernels, cross_attend(): pl.pallas_call(cross_kernel, out_shape=(jax.ShapeDtypeStruct((rows, width...  7.76 us

profile of v2, /device:TPU:0, one launch (start us, length us, event | category | flops | bytes accessed | tf_op | source)
XLA Modules:
  0.0 95.8 jit_solution(6609309366022442775)
XLA Ops:
  0.0 0.0 copy-start.6
  0.0 0.9 copy-done.6
  0.9 0.0 copy-start.7
  0.9 0.7 copy-done.7
  1.6 25.8 %gather_frames.1 = (bf16[16,128,512]{2,1,0:T(8,128)(2,1)S(1)}, s32[16,8,128]{2,1,0:T(8,128)S(1)}) custom-call(bf16[128,512]{1,0:T(8,128)(2,1)S(1)} %copy-done.6, s32[1,128]{1,0:T(1,128)S(1)} %bitcast.1), custom_call_target="tpu_custom_call" | custom-call | tf_op jit(solution)/shard_map/gather_frames/pallas_call | solution.py:271
  27.4 0.0 copy-start.1
  27.4 1.6 %copy-done.1 = bf16[512,2048]{1,0:T(8,128)(2,1)S(1)} copy-done((bf16[512,2048]{1,0:T(8,128)(2,1)S(1)}, bf16[512,2048]{1,0:T(8,128)(2,1)}, u32[]{:S(2)}) %copy-start.1) | copy-done | bytes 2097176
  29.0 0.0 copy-start.2
  29.0 1.6 %copy-done.2 = bf16[1024,1024]{1,0:T(8,128)(2,1)S(1)} copy-done((bf16[1024,1024]{1,0:T(8,128)(2,1)S(1)}, bf16[1024,1024]{1,0:T(8,128)(2,1)}, u32[]{:S(2)}) %copy-start.2) | copy-done | bytes 2097176
  30.6 0.0 copy-start.4
  30.6 0.9 copy-done.4
  31.5 0.0 copy-start.5
  31.5 0.9 copy-done.5
  32.5 0.0 copy-start
  32.5 7.8 %cross_attend.1 = (f32[128,1024]{1,0:T(8,128)S(1)}, bf16[128,1024]{1,0:T(8,128)(2,1)S(1)}) custom-call(s32[16,8,128]{2,1,0:T(8,128)S(1)} %get-tuple-element.9.ids, bf16[16,128,512]{2,1,0:T(8,128)(2,1)S(1)} %get-tuple-element.10.every, bf16[128,1024]{1,0:T(8,128)(2,1)S(1)} %copy-done.4, bf16[128,1024]{1,0:T(8,128)(2,1)S(1)} %copy-done.5, ...), custom_call_target="tpu_custom_call" | custom-call | tf_op jit(solution)/shard_map/cross_attend/pallas_call | solution.py:415
  40.2 0.0 copy-done
  40.2 0.0 copy-start.3
  40.3 1.6 %copy-done.3 = bf16[1024,1024]{1,0:T(8,128)(2,1)S(1)} copy-done((bf16[1024,1024]{1,0:T(8,128)(2,1)S(1)}, bf16[1024,1024]{1,0:T(8,128)(2,1)}, u32[]{:S(2)}) %copy-start.3) | copy-done | bytes 2097176
  41.8 53.3 %self_attend.1 = bf16[128,1024]{1,0:T(8,128)(2,1)S(1)} custom-call(bf16[128,1024]{1,0:T(8,128)(2,1)S(1)} %get-tuple-element.11.normed, f32[128,1024]{1,0:T(8,128)S(1)} %get-tuple-element.12.mixed, bf16[1024,3072]{1,0:T(8,128)(2,1)S(1)} %copy-done, bf16[1024,1024]{1,0:T(8,128)(2,1)S(1)} %copy-done.3), custom_call_target="tpu_custom_call" | custom-call | tf_op jit(solution)/shard_map/self_attend/pallas_call | solution.py:540
  95.1 0.7 copy.10
Async XLA Ops:
  0.0 0.9 copy-start.6
  0.9 0.7 copy-start.7
  27.4 1.6 %copy-start.1 = (bf16[512,2048]{1,0:T(8,128)(2,1)S(1)}, bf16[512,2048]{1,0:T(8,128)(2,1)}, u32[]{:S(2)}) copy-start(bf16[512,2048]{1,0:T(8,128)(2,1)} %w_kv.1) | copy-start | bytes 6291460
  29.0 1.6 %copy-start.2 = (bf16[1024,1024]{1,0:T(8,128)(2,1)S(1)}, bf16[1024,1024]{1,0:T(8,128)(2,1)}, u32[]{:S(2)}) copy-start(bf16[1024,1024]{1,0:T(8,128)(2,1)} %w_out.2) | copy-start | bytes 6291460
  30.6 0.9 copy-start.4
  31.5 0.9 copy-start.5
  32.5 7.8 %copy-start = (bf16[1024,3072]{1,0:T(8,128)(2,1)S(1)}, bf16[1024,3072]{1,0:T(8,128)(2,1)}, u32[]{:S(2)}) copy-start(bf16[1024,3072]{1,0:T(8,128)(2,1)} %w_qkv.1) | copy-start | bytes 18874372
  40.2 1.6 %copy-start.3 = (bf16[1024,1024]{1,0:T(8,128)(2,1)S(1)}, bf16[1024,1024]{1,0:T(8,128)(2,1)}, u32[]{:S(2)}) copy-start(bf16[1024,1024]{1,0:T(8,128)(2,1)} %w_out.3) | copy-start | bytes 6291460

commit v3 on v2

--- a/solution.py
+++ b/solution.py
@@ -216,12 +216,16 @@
 
 
 def gather_kernel(
-    frames, seg, every, ids, seg8, send_up, send_down, send_x, send_core, recv, seg_send, seg_recv, local
+    frames, seg, every, ids, seg1, seg8, send_up, send_down, send_x, send_core, recv, seg_send,
+    seg_recv, local
 ):
     place = Place()
     me = place.me
     barrier = greet([(lax.rem(me + d, 16), None) for d in range(1, 16)])
-    seg8[...] = jnp.broadcast_to(seg[...], seg8.shape)
+    load = pltpu.make_async_copy(seg, seg1, local.at[2])
+    load.start()
+    load.wait()
+    seg8[...] = jnp.broadcast_to(seg1[...], seg8.shape)
     own = pltpu.make_async_copy(frames, every.at[me], local.at[0])
     own.start()
     own_ids = pltpu.make_async_copy(seg8, ids.at[me], local.at[1])
@@ -274,9 +278,10 @@
             jax.ShapeDtypeStruct((16, rows, channels), frames.dtype),
             jax.ShapeDtypeStruct((16, 8, rows), jnp.int32),
         ),
-        in_specs=[pl.BlockSpec(memory_space=pl.ANY), pl.BlockSpec(memory_space=pltpu.VMEM)],
+        in_specs=[pl.BlockSpec(memory_space=pl.ANY)] * 2,
         out_specs=[pl.BlockSpec(memory_space=pl.ANY)] * 2,
         scratch_shapes=[
+            pltpu.VMEM((1, rows), jnp.int32),
             pltpu.VMEM((8, rows), jnp.int32),
             dma((4,)),
             dma((4,)),
@@ -285,10 +290,10 @@
             dma((16,)),
             dma((16,)),
             dma((16,)),
-            dma((2,)),
+            dma((3,)),
         ],
         compiler_params=pltpu.CompilerParams(
-            collective_id=0, has_side_effects=True, vmem_limit_bytes=4 * 2**20
+            collective_id=0, has_side_effects=True, vmem_limit_bytes=62 * 2**20
         ),
         name="gather_frames",
     )(frames, segment.reshape(1, rows))
@@ -308,23 +313,37 @@
     acc[...] = jnp.zeros(acc.shape, jnp.float32)
 
 
-def attend(p, query, key, value, peak, total, acc, keep=None):
-    score = lax.dot_general(
-        query, key, (((1,), (1,)), ((), ())), preferred_element_type=jnp.float32
-    )
+def attend(pairs, queries, keys, values, peak, total, acc, keep=None):
+    scores = [
+        lax.dot_general(query, key, (((1,), (1,)), ((), ())), preferred_element_type=jnp.float32)
+        for query, key in zip(queries, keys)
+    ]
     if keep is not None:
-        column = lax.broadcasted_iota(jnp.int32, score.shape, 1)
-        score = jnp.where(column < keep, score, -jnp.inf)
-    before = peak[p]
-    now = jnp.maximum(before, jnp.max(score, axis=1, keepdims=True))
-    half = now.shape[1]
-    left = jnp.exp(score[:, :half] - now)
-    right = jnp.exp(score[:, half:] - now)
-    fade = jnp.exp(before - now)
-    peak[p] = now
-    total[p] = total[p] * fade + (left + right)
-    weights = jnp.concatenate([left.astype(jnp.bfloat16), right.astype(jnp.bfloat16)], axis=1)
-    acc[p] = acc[p] * fade + jnp.dot(weights, value, preferred_element_type=jnp.float32)
+        column = lax.broadcasted_iota(jnp.int32, scores[0].shape, 1)
+        scores = [jnp.where(column < keep, score, -jnp.inf) for score in scores]
+    before = [peak[p] for p in pairs]
+    old_total = [total[p] for p in pairs]
+    old_acc = [acc[p] for p in pairs]
+    now = [
+        jnp.maximum(b, jnp.max(score, axis=1, keepdims=True)) for b, score in zip(before, scores)
+    ]
+    half = now[0].shape[1]
+    left = [jnp.exp(score[:, :half] - n) for score, n in zip(scores, now)]
+    right = [jnp.exp(score[:, half:] - n) for score, n in zip(scores, now)]
+    fade = [jnp.exp(b - n) for b, n in zip(before, now)]
+    weights = [
+        jnp.concatenate([a.astype(jnp.bfloat16), b.astype(jnp.bfloat16)], axis=1)
+        for a, b in zip(left, right)
+    ]
+    added = [
+        jnp.dot(w, value, preferred_element_type=jnp.float32) for w, value in zip(weights, values)
+    ]
+    new_total = [t * f + (a + b) for t, f, a, b in zip(old_total, fade, left, right)]
+    new_acc = [o * f + a for o, f, a in zip(old_acc, fade, added)]
+    for position, p in enumerate(pairs):
+        peak[p] = now[position]
+        total[p] = new_total[position]
+        acc[p] = new_acc[position]
 
 
 def join_pair(p, total, acc):
@@ -339,9 +358,17 @@
 
 
 def cross_kernel(
-    ids, every, queries, latents, w_kv, w_out, mixed, normed, block, keyval, query, peak, total,
-    acc, cross, chosen, sems
+    ids, every, queries_all, latents_all, w_kv_all, w_out_all, mixed, normed, block, keyval, query,
+    peak, total, acc, cross, queries, latents, w_kv, w_out, chosen, sems, local
 ):
+    loads = [
+        pltpu.make_async_copy(src, dst, local.at[n])
+        for n, (src, dst) in enumerate(
+            [(queries_all, queries), (w_kv_all, w_kv), (w_out_all, w_out), (latents_all, latents)]
+        )
+    ]
+    for load in loads[:2]:
+        load.start()
     wanted = lax.axis_index("frame") // 2 + 1
     width = queries.shape[1]
     scale = 1.0 / math.sqrt(HEAD_DIM)
@@ -369,9 +396,13 @@
                 fetch(group, j).start()
 
     fetch_all(0)
+    for load in loads[2:]:
+        load.start()
+    loads[0].wait()
     for p in range(PAIRS):
         query[p] = split_pair(queries[:, p * 128 : p * 128 + 128] * scale)
     clear(peak, total, acc)
+    loads[1].wait()
 
     @pl.loop(0, (count + 3) // 4)
     def _(group):
@@ -393,15 +424,24 @@
         fetch_all(group + 1)
         keep = (count - group * 4) * 64
 
-        @pl.loop(0, PAIRS, unroll=2)
-        def _(p):
+        @pl.loop(0, PAIRS // 4)
+        def _(group):
+            pairs = [group * 4 + i for i in range(4)]
             attend(
-                p, query[p], keyval[:, pair_columns(p)], keyval[:, pair_columns(p + PAIRS)],
-                peak, total, acc, keep,
+                pairs,
+                [query[p] for p in pairs],
+                [keyval[:, pair_columns(p)] for p in pairs],
+                [keyval[:, pair_columns(p + PAIRS)] for p in pairs],
+                peak,
+                total,
+                acc,
+                keep,
             )
 
     for p in range(PAIRS):
         cross[:, p * 128 : p * 128 + 128] = join_pair(p, total, acc)
+    loads[2].wait()
+    loads[3].wait()
     whole = latents[...].astype(jnp.float32) + jnp.dot(
         cross[...], w_out[...], preferred_element_type=jnp.float32
     )
@@ -420,11 +460,7 @@
         ),
         in_specs=[
             pl.BlockSpec(memory_space=pltpu.SMEM),
-            pl.BlockSpec(memory_space=pl.ANY),
-            vmem,
-            vmem,
-            vmem,
-            vmem,
+            *[pl.BlockSpec(memory_space=pl.ANY)] * 5,
         ],
         out_specs=[vmem, vmem],
         scratch_shapes=[
@@ -435,10 +471,15 @@
             pltpu.VMEM((PAIRS, 2 * rows, 128), jnp.float32),
             pltpu.VMEM((PAIRS, 2 * rows, 128), jnp.float32),
             pltpu.VMEM((rows, width), jnp.bfloat16),
+            pltpu.VMEM(queries.shape, jnp.bfloat16),
+            pltpu.VMEM(latents.shape, jnp.bfloat16),
+            pltpu.VMEM(w_kv.shape, jnp.bfloat16),
+            pltpu.VMEM(w_out.shape, jnp.bfloat16),
             pltpu.SMEM((64,), jnp.int32),
             pltpu.SemaphoreType.DMA((4,)),
+            pltpu.SemaphoreType.DMA((4,)),
         ],
-        compiler_params=pltpu.CompilerParams(vmem_limit_bytes=24 * 2**20),
+        compiler_params=pltpu.CompilerParams(vmem_limit_bytes=61 * 2**20),
         name="cross_attend",
     )(ids, every, queries, latents, w_kv, w_out)
 
@@ -511,11 +552,21 @@
         theirs = keyval.at[chip, 1 - place.core]
         push(theirs, theirs, send_core.at[step], recv_core.at[step], place.sibling).wait_recv()
 
-        @pl.loop(0, PAIRS, unroll=2)
-        def _(p):
-            key = keyval[chip, :, :, pair_columns(p)].reshape(2 * rows, 128)
-            value = keyval[chip, :, :, pair_columns(p + PAIRS)].reshape(2 * rows, 128)
-            attend(p, query[p], key, value, peak, total, acc)
+        @pl.loop(0, PAIRS // 4)
+        def _(group):
+            pairs = [group * 4 + i for i in range(4)]
+            attend(
+                pairs,
+                [query[p] for p in pairs],
+                [keyval[chip, :, :, pair_columns(p)].reshape(2 * rows, 128) for p in pairs],
+                [
+                    keyval[chip, :, :, pair_columns(p + PAIRS)].reshape(2 * rows, 128)
+                    for p in pairs
+                ],
+                peak,
+                total,
+                acc,
+            )
 
     chip = take(0)
     for step in range(1, len(STEPS)):
@@ -561,7 +612,7 @@
             dma((2,)),
         ],
         compiler_params=pltpu.CompilerParams(
-            collective_id=1, has_side_effects=True, vmem_limit_bytes=40 * 2**20
+            collective_id=1, has_side_effects=True, vmem_limit_bytes=60 * 2**20
         ),
         name="self_attend",
     )(normed, mixed, w_qkv, w_out)

time: 94.9 us -> 78.6 us (0.83); the launches traced: 95.8 us -> 77.1 us
  Pallas kernels: 86.8 us -> 75.4 us
  local copies, waits for them, and re-layouts: 8.93 us -> 1.67 us
    pallas_call x1, Pallas kernels: 53.3 us -> 40.4 us  [self_attend(): pl.pallas_call(self_kernel, out_shape=jax.ShapeDtypeStruct((rows, width),...]
    unnamed x17 -> x1, local copies, waits for them, and re-layouts: 8.93 us -> 1.67 us
    pallas_call x1, Pallas kernels: 25.8 us -> 27 us  [gather_frames(): pl.pallas_call(gather_kernel, out_shape=(jax.ShapeDtypeStruct((16, rows,...]
where the time goes in v3:
time: 78.6 us; the launch traced here: 77.1 us
  Pallas kernels  75.4 us (96%)
  local copies, waits for them, and re-layouts  1.67 us (2%)
    pallas_call x1, Pallas kernels, self_attend(): pl.pallas_call(self_kernel, out_shape=jax.ShapeDtypeStruct((rows, width),...  40.4 us
    pallas_call x1, Pallas kernels, gather_frames(): pl.pallas_call(gather_kernel, out_shape=(jax.ShapeDtypeStruct((16, rows,...  27 us
    pallas_call x1, Pallas kernels, cross_attend(): pl.pallas_call(cross_kernel, out_shape=(jax.ShapeDtypeStruct((rows, width...  8.02 us
    unnamed x1, local copies, waits for them, and re-layouts  1.67 us

profile of v3, /device:TPU:0, one launch (start us, length us, event | category | flops | bytes accessed | tf_op | source)
XLA Modules:
  0.0 77.1 jit_solution(14181835923349200328)
XLA Ops:
  0.0 27.0 %gather_frames.1 = (bf16[16,128,512]{2,1,0:T(8,128)(2,1)}, s32[16,8,128]{2,1,0:T(8,128)}) custom-call(bf16[128,512]{1,0:T(8,128)(2,1)} %frames.1, s32[1,128]{1,0:T(1,128)} %bitcast.1), custom_call_target="tpu_custom_call" | custom-call | tf_op jit(solution)/shard_map/gather_frames/pallas_call | solution.py:275
  27.1 8.0 %cross_attend.1 = (f32[128,1024]{1,0:T(8,128)}, bf16[128,1024]{1,0:T(8,128)(2,1)}) custom-call(s32[16,8,128]{2,1,0:T(8,128)} %get-tuple-element.9.ids, bf16[16,128,512]{2,1,0:T(8,128)(2,1)} %get-tuple-element.10.every, bf16[128,1024]{1,0:T(8,128)(2,1)} %queries_all.1, bf16[128,1024]{1,0:T(8,128)(2,1)} %latents_all.1, bf16[512,2048]{1,0:T(8,128)(2,1)} %w_kv_all.1, ...), custom_call_target="tpu_custom_call" | custom-call | tf_op jit(solution)/shard_map/cross_attend/pallas_call | solution.py:455
  35.1 40.4 %self_attend.1 = bf16[128,1024]{1,0:T(8,128)(2,1)} custom-call(bf16[128,1024]{1,0:T(8,128)(2,1)} %get-tuple-element.11.normed, f32[128,1024]{1,0:T(8,128)} %get-tuple-element.12.mixed, bf16[1024,3072]{1,0:T(8,128)(2,1)} %w_qkv.1, bf16[1024,1024]{1,0:T(8,128)(2,1)} %w_out.1), custom_call_target="tpu_custom_call" | custom-call | tf_op jit(solution)/shard_map/self_attend/pallas_call | solution.py:591
  75.5 1.7 %copy.10 = bf16[128,1024]{1,0:T(8,128)(2,1)} copy(bf16[128,1024]{1,0:T(8,128)(2,1)} %self_attend.1) | data formatting | bytes 524288
